TPU v7x, 1024 devices: a whole 4x8x16 slice. The times are simulated.
1024 devices in a mesh: dp: 64 (over y, x, core), fsdp: 16 (over z).
Axes of the slice: x: 4, y: 8, z: 16, core: 2. Of those that a mesh axis runs over, the one named last changes fastest.
Arguments:
- grad_partial: bfloat16 [64, 16, 64, 2048], P('dp', None, None, 'fsdp'), may hold values from -16 to 16
- weights: bfloat16 [16, 64, 2048], P(None, None, 'fsdp'), may hold values from -0.59765625 to 0.59765625
- momentum: float32 [16, 4, 64, 2048], P('fsdp'), may hold values from -6 to 6
- owners: int32 [16], replicated, may hold values from 0 to 15, as said below
Outputs:
- weights_out: bfloat16 [16, 64, 2048], replicated
- momentum_out: float32 [16, 4, 64, 2048], P('fsdp')
Inputs may be any that keep to these rules, and one draw needn't show every extreme that they name: `owners`: no owner holds more than 4 matrices, and one owner holds exactly 4.
All inputs are finite; a program needn't handle non-finite values.
Results may differ from a plain program's by a relative error of at most 0.013.
Values may be sent and summed in bfloat16 or wider, within the bound.
No kernel may reach another device: no remote copies, remote signals or barrier semaphores. Data moves between devices by JAX's collectives and lax.ppermute only.
A program may use at most 32 MiB of HBM per device.

v0:
```python
import jax
import jax.numpy as jnp
from jax import lax
from jax.experimental import pallas as pl
from jax.experimental.pallas import tpu as pltpu
from jax.sharding import Mesh, PartitionSpec as P

E = 64
D = 2048
L = 16
DEPTH = 4
ITERS = 5
NY, NX, NC, NZ = 8, 4, 2, 16
HALF = L // NC
RG = 4
ROWS = E // RG
COLS = D // NZ
GROUP = 4 * E
DP = ("y", "x", "core")
Z = "fsdp"

coef_a = 3.4445
coef_b = -4.775
coef_c = 2.0315
moment_rate = 0.95
learn_rate = 0.1
decay_rate = 0.1
scale = 0.2 * D**0.5
INIT_S = 1.0 + moment_rate
INIT_M = moment_rate * moment_rate
BACK_I = 1.0 / INIT_S
BACK_M = moment_rate - INIT_M / INIT_S


def split(a):
    high = a.astype(jnp.bfloat16)
    return high, (a - high.astype(jnp.float32)).astype(jnp.bfloat16)


def dot(a, b):
    return jnp.dot(a, b, preferred_element_type=jnp.float32)


def assemble_kernel(index_ref, own_ref, *refs):
    *pieces, xs, near_ref = refs
    pieces = [(ref, 0, 1 + k // 2, k % 2) for k, ref in enumerate(pieces)]
    pieces += [(own_ref, part * RG, 0, part) for part in range(2)]
    for ref, at, place, part in pieces:
        layer = 2 * index_ref[place] + part
        for z in range(NZ):
            xs[layer, :, z * COLS : (z + 1) * COLS] = ref[at : at + RG, z].reshape(E, COLS)
    for s in range(DEPTH):
        near_ref[s] = xs[index_ref[NX + s]]


def assemble(index, own, *others):
    vmem = pl.BlockSpec(memory_space=pltpu.VMEM)
    return pl.pallas_call(
        assemble_kernel,
        out_shape=(
            jax.ShapeDtypeStruct((HALF, E, D), jnp.bfloat16),
            jax.ShapeDtypeStruct((DEPTH, E, D), jnp.bfloat16),
        ),
        in_specs=[pl.BlockSpec(memory_space=pltpu.SMEM), vmem] + [vmem] * len(others),
        out_specs=(vmem, vmem),
        compiler_params=pltpu.CompilerParams(vmem_limit_bytes=16 * 2**20),
        cost_estimate=pl.CostEstimate(flops=0, bytes_accessed=4 * 2**20, transcendentals=0),
        name="assemble",
    )(index, own, *others)


def poly_kernel(xs, high_ref, low_ref):
    row = lax.broadcasted_iota(jnp.int32, (GROUP, GROUP), 0)
    col = lax.broadcasted_iota(jnp.int32, (GROUP, GROUP), 1)
    same = (row >> 6) == (col >> 6)
    diagonal = row == col
    eye_a = jnp.where(diagonal, coef_a, 0.0)

    def mm(a, b):
        return dot(a[0], b[0]) + (dot(a[0], b[1]) + dot(a[1], b[0]))

    groups = range(HALF * E // GROUP)
    grams, scales = [], []
    for g in groups:
        x = xs[g * GROUP : (g + 1) * GROUP, :]
        gram = lax.dot_general(
            x, x, (((1,), (1,)), ((), ())), preferred_element_type=jnp.float32
        )
        trace = jnp.where(diagonal, gram, 0.0)
        by_row = jnp.sum(trace, axis=1, keepdims=True)
        by_col = jnp.sum(trace, axis=0, keepdims=True)
        total_row = jnp.sum(jnp.where(same, by_col, 0.0), axis=1, keepdims=True)
        total_col = jnp.sum(jnp.where(same, by_row, 0.0), axis=0, keepdims=True)
        inv_row = 1.0 / (jnp.sqrt(total_row) + 1e-07)
        inv_col = 1.0 / (jnp.sqrt(total_col) + 1e-07)
        grams.append(jnp.where(same, gram * inv_row * inv_col, 0.0))
        scales.append(inv_col)
    polys = [None for _ in groups]
    for repeat in range(ITERS):
        gram_parts = [split(gram) for gram in grams]
        squares = [mm(gram, gram) for gram in gram_parts]
        steps = [eye_a + coef_b * gram + coef_c * sq for gram, sq in zip(grams, squares)]
        step_parts = [split(step) for step in steps]
        if repeat < ITERS - 1:
            halfway = [split(mm(step, gram)) for step, gram in zip(step_parts, gram_parts)]
            grams = [mm(half, step) for half, step in zip(halfway, step_parts)]
        polys = [
            step if poly is None else mm(part, split(poly))
            for step, part, poly in zip(steps, step_parts, polys)
        ]
    for g in groups:
        high_ref[g], low_ref[g] = split(polys[g] * scales[g])


def polynomials(x):
    vmem = pl.BlockSpec(memory_space=pltpu.VMEM)
    poly = jax.ShapeDtypeStruct((HALF * E // GROUP, GROUP, GROUP), jnp.bfloat16)
    return pl.pallas_call(
        poly_kernel,
        out_shape=(poly, poly),
        in_specs=[vmem],
        out_specs=(vmem, vmem),
        compiler_params=pltpu.CompilerParams(vmem_limit_bytes=16 * 2**20),
        cost_estimate=pl.CostEstimate(
            flops=8 * 10**9, bytes_accessed=4 * 2**20, transcendentals=0
        ),
        name="polynomials",
    )(x)


def weights_kernel(xs, high_ref, low_ref, w_ref, half_ref):
    for g in range(HALF * E // GROUP):
        high, low = high_ref[g], low_ref[g]
        for z in range(NZ // 2):
            x = xs[g * GROUP : (g + 1) * GROUP, 2 * z * COLS : 2 * (z + 1) * COLS]
            ortho = dot(high, x) + dot(low, x)
            for part in range(2):
                k = 2 * z + part
                wide = w_ref[k, 4 * g : 4 * (g + 1)].reshape(GROUP, COLS).astype(jnp.float32)
                mine = ortho[:, part * COLS : (part + 1) * COLS]
                new = wide - learn_rate * (scale * mine + decay_rate * wide)
                half_ref[4 * g : 4 * (g + 1), :, k * COLS : (k + 1) * COLS] = new.astype(
                    jnp.bfloat16
                ).reshape(4, E, COLS)


def update_weights(xs, high, low, weights):
    vmem = pl.BlockSpec(memory_space=pltpu.VMEM)
    return pl.pallas_call(
        weights_kernel,
        out_shape=jax.ShapeDtypeStruct((HALF, E, D), jnp.bfloat16),
        in_specs=[vmem, vmem, vmem, vmem],
        out_specs=vmem,
        compiler_params=pltpu.CompilerParams(vmem_limit_bytes=16 * 2**20),
        cost_estimate=pl.CostEstimate(
            flops=2 * 10**9, bytes_accessed=6 * 2**20, transcendentals=0
        ),
        name="update_weights",
    )(xs, high, low, weights)


def join_kernel(core_ref, other_ref, mine_ref, full_ref, sem):
    del mine_ref
    base = (NC - 1 - core_ref[0]) * HALF
    copies = [
        pltpu.make_async_copy(
            other_ref.at[pl.ds(2 * k, 2)], full_ref.at[pl.ds(base + 2 * k, 2)], sem.at[k]
        )
        for k in range(HALF // 2)
    ]
    for copy in copies:
        copy.start()
    for copy in copies:
        copy.wait()


def join_halves(core, other, full):
    hbm = pl.BlockSpec(memory_space=pltpu.HBM)
    return pl.pallas_call(
        join_kernel,
        out_shape=jax.ShapeDtypeStruct((L, E, D), jnp.bfloat16),
        in_specs=[
            pl.BlockSpec(memory_space=pltpu.SMEM),
            pl.BlockSpec(memory_space=pltpu.VMEM),
            hbm,
        ],
        out_specs=hbm,
        input_output_aliases={2: 0},
        scratch_shapes=[pltpu.SemaphoreType.DMA((HALF // 2,))],
        compiler_params=pltpu.CompilerParams(vmem_limit_bytes=8 * 2**20),
        name="join_halves",
    )(core, other, full)


def moment_kernel(
    core_ref, source_ref, half_ref, near_ref, far_ref, m_ref, o_ref, full_ref, ms, sem, half_sem
):
    base = core_ref[0] * HALF
    copies = [
        pltpu.make_async_copy(
            half_ref.at[pl.ds(2 * k, 2)], full_ref.at[pl.ds(base + 2 * k, 2)], half_sem.at[k]
        )
        for k in range(HALF // 2)
    ]
    for copy in copies:
        copy.start()
    for s in range(DEPTH):
        source = source_ref[s]
        for z in range(NZ):
            columns = slice(z * COLS, (z + 1) * COLS)
            near = near_ref[s, :, columns].astype(jnp.float32)
            far = far_ref[s, :, columns].astype(jnp.float32)
            initial = jnp.where(source == 1, near, far)
            moment = BACK_I * initial + BACK_M * m_ref[s, :, columns]
            ms[s, :, columns] = jnp.where(source > 0, moment, 0.0)
        copy = pltpu.make_async_copy(ms.at[s], o_ref.at[s], sem.at[s])
        copy.start()
        copies.append(copy)
    for copy in copies:
        copy.wait()


def update_momentum(core, source, half, near, far, momentum):
    smem = pl.BlockSpec(memory_space=pltpu.SMEM)
    vmem = pl.BlockSpec(memory_space=pltpu.VMEM)
    hbm = pl.BlockSpec(memory_space=pltpu.HBM)
    return pl.pallas_call(
        moment_kernel,
        out_shape=(
            jax.ShapeDtypeStruct((DEPTH, E, D), jnp.float32),
            jax.ShapeDtypeStruct((L, E, D), jnp.bfloat16),
        ),
        in_specs=[smem, smem, vmem, vmem, vmem, vmem],
        out_specs=(hbm, hbm),
        scratch_shapes=[
            pltpu.VMEM((DEPTH, E, D), jnp.float32),
            pltpu.SemaphoreType.DMA((DEPTH,)),
            pltpu.SemaphoreType.DMA((HALF // 2,)),
        ],
        compiler_params=pltpu.CompilerParams(vmem_limit_bytes=16 * 2**20),
        cost_estimate=pl.CostEstimate(
            flops=4 * 10**6, bytes_accessed=10 * 2**20, transcendentals=0
        ),
        name="update_momentum",
    )(core, source, half, near, far, momentum)


def spread(x, axis, count):
    return lax.all_to_all(jnp.broadcast_to(x[None], (count,) + x.shape), axis, 0, 0, tiled=True)


def local(grad_partial, weights, momentum, owners):
    y, x, core = lax.axis_index("y"), lax.axis_index("x"), lax.axis_index("core")
    own_index = lax.axis_index(Z)
    layers = jnp.arange(L, dtype=jnp.int32)
    first = HALF * core
    slots = jnp.sum(
        ((owners[None, :] == owners[:, None]) & (layers[None, :] < layers[:, None])).astype(
            jnp.int32
        ),
        axis=1,
    )

    kept = lax.dynamic_slice_in_dim(weights, first, HALF, 0)
    weights_half = lax.all_gather(kept, Z)

    my_layer = first + 2 * x + y // RG
    my_rows = (y % RG) * ROWS
    my_owner = lax.dynamic_index_in_dim(owners, my_layer, 0, keepdims=False)
    my_slot = lax.dynamic_index_in_dim(slots, my_layer, 0, keepdims=False)

    held = lax.dynamic_slice(momentum[0], (my_slot, my_rows, 0), (1, ROWS, D))[0]
    held = held.astype(jnp.bfloat16).reshape(ROWS, NZ, COLS).transpose(1, 0, 2)
    previous = lax.all_to_all(held, Z, 0, 0, tiled=True)
    previous = lax.dynamic_index_in_dim(previous, my_owner, 0, keepdims=False).astype(jnp.float32)

    outgoing = grad_partial[0].reshape(L * RG, ROWS, COLS)
    arrived = lax.all_to_all(outgoing, ("core", "x", "y"), 0, 0, tiled=True)
    summed = jnp.sum(arrived.astype(jnp.float32), axis=0)
    initial = INIT_S * summed + INIT_M * previous

    block = spread(initial.astype(jnp.bfloat16), Z, NZ)
    block = spread(block, "y", NY)
    ahead = [(k, (k + 1) % NX) for k in range(NX)]
    back = [(k, (k - 1) % NX) for k in range(NX)]
    left0 = lax.ppermute(block[:RG], "x", ahead)
    right1 = lax.ppermute(block[RG:], "x", back)
    left0, second_half = lax.optimization_barrier((left0, block[RG:]))
    far0 = lax.ppermute(left0, "x", ahead)
    left1 = lax.ppermute(second_half, "x", ahead)
    right1, first_half = lax.optimization_barrier((right1, block[:RG]))
    far1 = lax.ppermute(right1, "x", back)
    right0 = lax.ppermute(first_half, "x", back)

    hits = (owners[None, :] == own_index) & (
        slots[None, :] == jnp.arange(DEPTH, dtype=jnp.int32)[:, None]
    )
    present = jnp.sum(hits.astype(jnp.int32), axis=1)
    which = jnp.sum(hits.astype(jnp.int32) * layers[None, :], axis=1)
    in_half = (which >= first) & (which < first + HALF)
    source = jnp.where(present > 0, jnp.where(in_half, 1, 2), 0).astype(jnp.int32)
    far0, far1, weights_half = lax.optimization_barrier((far0, far1, weights_half))
    places = (x + jnp.array([0, NX - 1, 2, 1], jnp.int32)) % NX
    index = jnp.concatenate([places, which % HALF]).astype(jnp.int32)
    xs, near = assemble(index, block, left0, left1, far0, far1, right0, right1)

    where = core.astype(jnp.int32)[None]
    xs, near = lax.optimization_barrier((xs, near))
    xs = xs.reshape(HALF * E, D)
    far = lax.ppermute(near, "core", [(0, 1), (1, 0)])
    high, low = polynomials(xs)
    high, low, far = lax.optimization_barrier((high, low, far))
    half = update_weights(xs, high, low, weights_half)
    other = lax.ppermute(half, "core", [(0, 1), (1, 0)])
    moment, full = update_momentum(where, source, half, near, far, momentum[0])
    weights_out = join_halves(where, other, full)
    return (weights_out, moment[None])


def solution(mesh):
    mesh = Mesh(mesh.devices.reshape(NY, NX, NC, NZ), ("y", "x", "core", "fsdp"))
    in_specs = (
        P(DP, None, None, Z),
        P(None, None, Z),
        P(Z, None, None, None),
        P(),
    )
    out_specs = (P(), P(Z, None, None, None))
    return jax.shard_map(local, mesh=mesh, in_specs=in_specs, out_specs=out_specs, check_vma=False)
```

profile of v0, /device:TPU:1, one launch (start us, length us, event | category | flops | bytes accessed | tf_op | source)
XLA Modules:
  0.0 157.9 jit_solution(13178062325063617313)
XLA Ops:
  7.2 0.0 copy-start
  7.2 0.0 copy-start.3
  7.2 0.0 all-gather.3.cloned.1.call-start
  7.2 0.9 copy-done
  8.1 0.7 constant_dynamic-slice_fusion
  8.8 0.0 all-gather.3.cloned.1.call-update
  8.8 0.0 copy-start.4
  8.8 18.4 %all-to-all-start = ((bf16[64,16,128]{2,1,0:T(8,128)(2,1)}), bf16[64,16,128]{2,1,0:T(8,128)(2,1)S(1)}, u32[]{:S(2)}, u32[]{:S(2)}) async-start(bf16[64,16,128]{2,1,0:T(8,128)(2,1)} %bitcast.27), calls=%async_computation | async-start | bytes 524288 | tf_op jit(solution)/shard_map/all_to_all | solution.py:278
  27.3 0.9 convert_reduce_fusion.1
  28.2 0.6 dynamic_slice.17
  30.8 0.9 fusion
  31.7 0.6 copy.9
  32.3 8.3 %all-to-all-done = bf16[64,16,128]{2,1,0:T(8,128)(2,1)S(1)} async-done(((bf16[64,16,128]{2,1,0:T(8,128)(2,1)}), bf16[64,16,128]{2,1,0:T(8,128)(2,1)S(1)}, u32[]{:S(2)}, u32[]{:S(2)}) %all-to-all-start) | async-done | bytes 262176 | tf_op jit(solution)/shard_map/all_to_all | solution.py:278
  40.6 11.9 %all-to-all-start.1 = ((bf16[16,16,128]{2,1,0:T(8,128)(2,1)}), bf16[16,16,128]{2,1,0:T(8,128)(2,1)S(1)}, u32[]{:S(2)}, u32[]{:S(2)}) async-start(bf16[16,16,128]{2,1,0:T(8,128)(2,1)} %copy.9), calls=%async_computation.1 | async-start | bytes 131072 | tf_op jit(solution)/shard_map/all_to_all | solution.py:274
  52.5 1.3 dynamic_slice.19
  55.9 0.1 convert_reduce_fusion
  56.0 8.3 %all-to-all-done.1 = bf16[16,16,128]{2,1,0:T(8,128)(2,1)S(1)} async-done(((bf16[16,16,128]{2,1,0:T(8,128)(2,1)}), bf16[16,16,128]{2,1,0:T(8,128)(2,1)S(1)}, u32[]{:S(2)}, u32[]{:S(2)}) %all-to-all-start.1) | async-done | bytes 65568 | tf_op jit(solution)/shard_map/all_to_all | solution.py:274
  64.3 15.3 %all_to_all.20 = bf16[16,16,128]{2,1,0:T(8,128)(2,1)S(1)} all-to-all(bf16[16,16,128]{2,1,0:T(8,128)(2,1)S(1)} %broadcast_in_dim.22), channel_id=1, replica_groups=mesh['y'=8,'x'=4,'core'=2,'fsdp'=16] {'fsdp'}, dimensions={0} | all-to-all | bytes 131072 | tf_op jit(solution)/shard_map/all_to_all | solution.py:249
  79.6 0.9 broadcast_in_dim.23
  80.5 4.0 %all-to-all-start.3 = ((bf16[8,16,16,128]{3,2,1,0:T(8,128)(2,1)}), bf16[8,16,16,128]{3,2,1,0:T(8,128)(2,1)S(1)}, u32[]{:S(2)}, u32[]{:S(2)}) async-start(bf16[8,16,16,128]{3,2,1,0:T(8,128)(2,1)} %broadcast_in_dim.23), calls=%async_computation.3 | async-start | bytes 1048576 | tf_op jit(solution)/shard_map/all_to_all | solution.py:249
  84.5 0.0 copy-done.3
  84.5 14.4 %all-to-all-done.3.own_ref = bf16[8,16,16,128]{3,2,1,0:T(8,128)(2,1)S(1)} async-done(((bf16[8,16,16,128]{3,2,1,0:T(8,128)(2,1)}), bf16[8,16,16,128]{3,2,1,0:T(8,128)(2,1)S(1)}, u32[]{:S(2)}, u32[]{:S(2)}) %all-to-all-start.3) | async-done | bytes 524320 | tf_op jit(solution)/shard_map/all_to_all | solution.py:249
  98.9 4.9 %collective-permute-start.3 = (bf16[4,16,16,128]{3,2,1,0:T(8,128)(2,1)S(1)}, bf16[4,16,16,128]{3,2,1,0:T(8,128)(2,1)S(1)}, u32[]{:S(2)}, u32[]{:S(2)}) collective-permute-start(bf16[4,16,16,128]{3,2,1,0:T(8,128)(2,1)S(1)} %get-tuple-element.19), channel_id=1, source_target_pairs={{0,96},{32,0},{64,32},{96,64},{1,97},{33,1},{65,33},{97,65},{2,98}... | collective-permute-start | bytes 786440 | tf_op jit(solution)/shard_map/ppermute | solution.py:287
  103.8 1.9 %collective-permute-start = (bf16[4,16,16,128]{3,2,1,0:T(8,128)(2,1)S(1)}, bf16[4,16,16,128]{3,2,1,0:T(8,128)(2,1)S(1)}, u32[]{:S(2)}, u32[]{:S(2)}) collective-permute-start(bf16[4,16,16,128]{3,2,1,0:T(8,128)(2,1)S(1)} %get-tuple-element.23), channel_id=1, source_target_pairs={{0,32},{32,64},{64,96},{96,0},{1,33},{33,65},{65,97},{97,1},{2,34}... | collective-permute-start | bytes 786440 | tf_op jit(solution)/shard_map/ppermute | solution.py:286
  105.8 0.1 convert_reduce_fusion.2
  105.9 1.2 collective-permute-done.3.refs_5_
  107.1 5.0 %collective-permute-start.4 = (bf16[4,16,16,128]{3,2,1,0:T(8,128)(2,1)S(1)}, bf16[4,16,16,128]{3,2,1,0:T(8,128)(2,1)S(1)}, u32[]{:S(2)}, u32[]{:S(2)}) collective-permute-start(bf16[4,16,16,128]{3,2,1,0:T(8,128)(2,1)S(1)} %collective-permute-done.3.refs_5_), channel_id=1, source_target_pairs={{0,96},{32,0},{64,32},{96,64},{1,97},{33,1},{65,33},{97,65},{2,98}... | collective-permute-start | bytes 786440 | tf_op jit(solution)/shard_map/ppermute | solution.py:292
  112.2 0.0 collective-permute-done.refs_0_
  112.2 1.9 %collective-permute-start.2 = (bf16[4,16,16,128]{3,2,1,0:T(8,128)(2,1)S(1)}, bf16[4,16,16,128]{3,2,1,0:T(8,128)(2,1)S(1)}, u32[]{:S(2)}, u32[]{:S(2)}) collective-permute-start(bf16[4,16,16,128]{3,2,1,0:T(8,128)(2,1)S(1)} %collective-permute-done.refs_0_), channel_id=1, source_target_pairs={{0,32},{32,64},{64,96},{96,0},{1,33},{33,65},{65,97},{97,1},{2,34}... | collective-permute-start | bytes 786440 | tf_op jit(solution)/shard_map/ppermute | solution.py:289
  114.1 4.6 %collective-permute-start.5 = (bf16[4,16,16,128]{3,2,1,0:T(8,128)(2,1)S(1)}, bf16[4,16,16,128]{3,2,1,0:T(8,128)(2,1)S(1)}, u32[]{:S(2)}, u32[]{:S(2)}) collective-permute-start(bf16[4,16,16,128]{3,2,1,0:T(8,128)(2,1)S(1)} %get-tuple-element.23), channel_id=1, source_target_pairs={{0,96},{32,0},{64,32},{96,64},{1,97},{33,1},{65,33},{97,65},{2,98}... | collective-permute-start | bytes 786440 | tf_op jit(solution)/shard_map/ppermute | solution.py:293
  118.7 1.9 %collective-permute-start.1 = (bf16[4,16,16,128]{3,2,1,0:T(8,128)(2,1)S(1)}, bf16[4,16,16,128]{3,2,1,0:T(8,128)(2,1)S(1)}, u32[]{:S(2)}, u32[]{:S(2)}) collective-permute-start(bf16[4,16,16,128]{3,2,1,0:T(8,128)(2,1)S(1)} %get-tuple-element.19), channel_id=1, source_target_pairs={{0,32},{32,64},{64,96},{96,0},{1,33},{33,65},{65,97},{97,1},{2,34}... | collective-permute-start | bytes 786440 | tf_op jit(solution)/shard_map/ppermute | solution.py:290
  120.6 0.0 copy-done.4
  120.6 0.1 pad_add_fusion.index_ref
  120.7 0.0 collective-permute-done.4.refs_3_
  120.7 0.0 collective-permute-done.2.refs_2_
  120.7 2.4 %collective-permute-done.5.refs_4_ = bf16[4,16,16,128]{3,2,1,0:T(8,128)(2,1)S(1)} collective-permute-done((bf16[4,16,16,128]{3,2,1,0:T(8,128)(2,1)S(1)}, bf16[4,16,16,128]{3,2,1,0:T(8,128)(2,1)S(1)}, u32[]{:S(2)}, u32[]{:S(2)}) %collective-permute-start.5) | collective-permute-done | bytes 262176 | tf_op jit(solution)/shard_map/ppermute | solution.py:293
  123.1 5.3 %collective-permute-done.1.refs_1_ = bf16[4,16,16,128]{3,2,1,0:T(8,128)(2,1)S(1)} collective-permute-done((bf16[4,16,16,128]{3,2,1,0:T(8,128)(2,1)S(1)}, bf16[4,16,16,128]{3,2,1,0:T(8,128)(2,1)S(1)}, u32[]{:S(2)}, u32[]{:S(2)}) %collective-permute-start.1) | collective-permute-done | bytes 262176 | tf_op jit(solution)/shard_map/ppermute | solution.py:290
  128.5 1.0 assemble.1
  129.5 6.9 %collective-permute-start.6 = (bf16[4,64,2048]{2,1,0:T(8,128)(2,1)S(1)}, bf16[4,64,2048]{2,1,0:T(8,128)(2,1)S(1)}, u32[]{:S(2)}, u32[]{:S(2)}) collective-permute-start(bf16[4,64,2048]{2,1,0:T(8,128)(2,1)S(1)} %get-tuple-element.27.near_ref), channel_id=1, source_target_pairs={{0,16},{16,0},{1,17},{17,1},{2,18},{18,2},{3,19},{19,3},{4,20},{20... | collective-permute-start | bytes 3145736 | tf_op jit(solution)/shard_map/ppermute | solution.py:310
  136.3 5.5 %polynomials.1 = (bf16[2,256,256]{2,1,0:T(8,128)(2,1)S(1)}, bf16[2,256,256]{2,1,0:T(8,128)(2,1)S(1)}) custom-call(bf16[512,2048]{1,0:T(8,128)(2,1)S(1)} %bitcast.25), custom_call_target="tpu_custom_call" | custom-call | flops 8000000000 | bytes 4194304 | tf_op jit(solution)/shard_map/polynomials/pallas_call | solution.py:118
  141.9 0.0 collective-permute-done.6.far_ref
  141.9 0.0 copy-done.2
  141.9 0.0 copy-start.1
  141.9 1.7 %update_weights.1.half_ref = bf16[8,64,2048]{2,1,0:T(8,128)(2,1)S(1)} custom-call(bf16[512,2048]{1,0:T(8,128)(2,1)S(1)} %bitcast.26, bf16[2,256,256]{2,1,0:T(8,128)(2,1)S(1)} %get-tuple-element.28.high_ref, bf16[2,256,256]{2,1,0:T(8,128)(2,1)S(1)} %get-tuple-element.29.low_ref, bf16[16,8,64,128]{3,2,1,0:T(8,128)(2,1)S(1)} %bitcast.24), custom_call_target="tpu_custom_call" | custom-call | flops 2000000000 | bytes 6291456 | tf_op jit(solution)/shard_map/update_weights/pallas_call | solution.py:149
  143.6 1.9 %collective-permute-start.7 = (bf16[8,64,2048]{2,1,0:T(8,128)(2,1)S(1)}, bf16[8,64,2048]{2,1,0:T(8,128)(2,1)S(1)}, u32[]{:S(2)}, u32[]{:S(2)}) collective-permute-start(bf16[8,64,2048]{2,1,0:T(8,128)(2,1)S(1)} %update_weights.1.half_ref), channel_id=1, source_target_pairs={{0,16},{16,0},{1,17},{17,1},{2,18},{18,2},{3,19},{19,3},{4,20},{20... | collective-permute-start | bytes 6291464 | tf_op jit(solution)/shard_map/ppermute | solution.py:314
  145.6 2.6 %update_momentum.1 = (f32[4,64,2048]{2,1,0:T(8,128)}, bf16[16,64,2048]{2,1,0:T(8,128)(2,1)}) custom-call(s32[1]{0:T(128)} %bitcast.core_ref, s32[4]{0:T(128)S(1)} %get-tuple-element.38.source_ref, bf16[8,64,2048]{2,1,0:T(8,128)(2,1)S(1)} %update_weights.1.half_ref, bf16[4,64,2048]{2,1,0:T(8,128)(2,1)S(1)} %get-tuple-element.27.near_ref, ...), custom_call_target="tpu_custom_call" | custom-call | flops 4000000 | bytes 10485760 | tf_op jit(solution)/shard_map/update_momentum/pallas_call | solution.py:227
  148.2 1.5 collective-permute-done.7.other_ref
  149.7 1.3 join_halves.1
  (10 shorter events, 0.1 us)
Async XLA Ops:
  7.2 1.0 copy-start
  7.2 77.3 %copy-start.3 = (s32[16]{0:T(128)S(1)}, s32[16]{0:T(128)}, u32[]{:S(2)}) copy-start(s32[16]{0:T(128)} %param.8) | copy-start | bytes 196
  7.2 113.5 %all-gather.3.cloned.1.call-start = ((), (), s32[]{:S(2)}) async-start(), calls=%async_computation.4 | async-start | bytes 2228224 | tf_op jit(solution)/shard_map/all_gather | solution.py:265
  8.8 111.8 %copy-start.4 = (s32[4]{0:T(128)S(1)}, s32[4]{0:T(128)}, u32[]{:S(2)}) copy-start(s32[4]{0:T(128)} %constant.93.clone) | copy-start | bytes 52
  8.8 31.8 %all-to-all-start = ((bf16[64,16,128]{2,1,0:T(8,128)(2,1)}), bf16[64,16,128]{2,1,0:T(8,128)(2,1)S(1)}, u32[]{:S(2)}, u32[]{:S(2)}) async-start(bf16[64,16,128]{2,1,0:T(8,128)(2,1)} %bitcast.27), calls=%async_computation | async-start | bytes 524288 | tf_op jit(solution)/shard_map/all_to_all | solution.py:278
  40.6 23.6 %all-to-all-start.1 = ((bf16[16,16,128]{2,1,0:T(8,128)(2,1)}), bf16[16,16,128]{2,1,0:T(8,128)(2,1)S(1)}, u32[]{:S(2)}, u32[]{:S(2)}) async-start(bf16[16,16,128]{2,1,0:T(8,128)(2,1)} %copy.9), calls=%async_computation.1 | async-start | bytes 131072 | tf_op jit(solution)/shard_map/all_to_all | solution.py:274
  80.5 18.4 %all-to-all-start.3 = ((bf16[8,16,16,128]{3,2,1,0:T(8,128)(2,1)}), bf16[8,16,16,128]{3,2,1,0:T(8,128)(2,1)S(1)}, u32[]{:S(2)}, u32[]{:S(2)}) async-start(bf16[8,16,16,128]{3,2,1,0:T(8,128)(2,1)} %broadcast_in_dim.23), calls=%async_computation.3 | async-start | bytes 1048576 | tf_op jit(solution)/shard_map/all_to_all | solution.py:249
  98.9 8.2 %collective-permute-start.3 = (bf16[4,16,16,128]{3,2,1,0:T(8,128)(2,1)S(1)}, bf16[4,16,16,128]{3,2,1,0:T(8,128)(2,1)S(1)}, u32[]{:S(2)}, u32[]{:S(2)}) collective-permute-start(bf16[4,16,16,128]{3,2,1,0:T(8,128)(2,1)S(1)} %get-tuple-element.19), channel_id=1, source_target_pairs={{0,96},{32,0},{64,32},{96,64},{1,97},{33,1},{65,33},{97,65},{2,98}... | collective-permute-start | bytes 786440 | tf_op jit(solution)/shard_map/ppermute | solution.py:287
  103.8 8.3 %collective-permute-start = (bf16[4,16,16,128]{3,2,1,0:T(8,128)(2,1)S(1)}, bf16[4,16,16,128]{3,2,1,0:T(8,128)(2,1)S(1)}, u32[]{:S(2)}, u32[]{:S(2)}) collective-permute-start(bf16[4,16,16,128]{3,2,1,0:T(8,128)(2,1)S(1)} %get-tuple-element.23), channel_id=1, source_target_pairs={{0,32},{32,64},{64,96},{96,0},{1,33},{33,65},{65,97},{97,1},{2,34}... | collective-permute-start | bytes 786440 | tf_op jit(solution)/shard_map/ppermute | solution.py:286
  107.1 13.6 %collective-permute-start.4 = (bf16[4,16,16,128]{3,2,1,0:T(8,128)(2,1)S(1)}, bf16[4,16,16,128]{3,2,1,0:T(8,128)(2,1)S(1)}, u32[]{:S(2)}, u32[]{:S(2)}) collective-permute-start(bf16[4,16,16,128]{3,2,1,0:T(8,128)(2,1)S(1)} %collective-permute-done.3.refs_5_), channel_id=1, source_target_pairs={{0,96},{32,0},{64,32},{96,64},{1,97},{33,1},{65,33},{97,65},{2,98}... | collective-permute-start | bytes 786440 | tf_op jit(solution)/shard_map/ppermute | solution.py:292
  112.2 8.5 %collective-permute-start.2 = (bf16[4,16,16,128]{3,2,1,0:T(8,128)(2,1)S(1)}, bf16[4,16,16,128]{3,2,1,0:T(8,128)(2,1)S(1)}, u32[]{:S(2)}, u32[]{:S(2)}) collective-permute-start(bf16[4,16,16,128]{3,2,1,0:T(8,128)(2,1)S(1)} %collective-permute-done.refs_0_), channel_id=1, source_target_pairs={{0,32},{32,64},{64,96},{96,0},{1,33},{33,65},{65,97},{97,1},{2,34}... | collective-permute-start | bytes 786440 | tf_op jit(solution)/shard_map/ppermute | solution.py:289
  114.1 9.0 %collective-permute-start.5 = (bf16[4,16,16,128]{3,2,1,0:T(8,128)(2,1)S(1)}, bf16[4,16,16,128]{3,2,1,0:T(8,128)(2,1)S(1)}, u32[]{:S(2)}, u32[]{:S(2)}) collective-permute-start(bf16[4,16,16,128]{3,2,1,0:T(8,128)(2,1)S(1)} %get-tuple-element.23), channel_id=1, source_target_pairs={{0,96},{32,0},{64,32},{96,64},{1,97},{33,1},{65,33},{97,65},{2,98}... | collective-permute-start | bytes 786440 | tf_op jit(solution)/shard_map/ppermute | solution.py:293
  118.7 9.8 %collective-permute-start.1 = (bf16[4,16,16,128]{3,2,1,0:T(8,128)(2,1)S(1)}, bf16[4,16,16,128]{3,2,1,0:T(8,128)(2,1)S(1)}, u32[]{:S(2)}, u32[]{:S(2)}) collective-permute-start(bf16[4,16,16,128]{3,2,1,0:T(8,128)(2,1)S(1)} %get-tuple-element.19), channel_id=1, source_target_pairs={{0,32},{32,64},{64,96},{96,0},{1,33},{33,65},{65,97},{97,1},{2,34}... | collective-permute-start | bytes 786440 | tf_op jit(solution)/shard_map/ppermute | solution.py:290
  129.5 12.4 %collective-permute-start.6 = (bf16[4,64,2048]{2,1,0:T(8,128)(2,1)S(1)}, bf16[4,64,2048]{2,1,0:T(8,128)(2,1)S(1)}, u32[]{:S(2)}, u32[]{:S(2)}) collective-permute-start(bf16[4,64,2048]{2,1,0:T(8,128)(2,1)S(1)} %get-tuple-element.27.near_ref), channel_id=1, source_target_pairs={{0,16},{16,0},{1,17},{17,1},{2,18},{18,2},{3,19},{19,3},{4,20},{20... | collective-permute-start | bytes 3145736 | tf_op jit(solution)/shard_map/ppermute | solution.py:310
  136.3 5.6 %copy-start.2 = (bf16[128,64,128]{2,1,0:T(8,128)(2,1)S(1)}, bf16[128,64,128]{2,1,0:T(8,128)(2,1)}, u32[]{:S(2)}) copy-start(bf16[128,64,128]{2,1,0:T(8,128)(2,1)} %all-gather.3.cloned.1.call-done) | copy-start | bytes 6291460
  141.9 3.7 %copy-start.1 = (f32[1,4,64,2048]{3,2,1,0:T(8,128)S(1)}, f32[1,4,64,2048]{3,2,1,0:T(8,128)}, u32[]{:S(2)}) copy-start(f32[1,4,64,2048]{3,2,1,0:T(8,128)} %param.7) | copy-start | bytes 6291460
  143.6 6.1 %collective-permute-start.7 = (bf16[8,64,2048]{2,1,0:T(8,128)(2,1)S(1)}, bf16[8,64,2048]{2,1,0:T(8,128)(2,1)S(1)}, u32[]{:S(2)}, u32[]{:S(2)}) collective-permute-start(bf16[8,64,2048]{2,1,0:T(8,128)(2,1)S(1)} %update_weights.1.half_ref), channel_id=1, source_target_pairs={{0,16},{16,0},{1,17},{17,1},{2,18},{18,2},{3,19},{19,3},{4,20},{20... | collective-permute-start | bytes 6291464 | tf_op jit(solution)/shard_map/ppermute | solution.py:314
Sparse Core Ops, SparseCore 0:
  11.3 79.5 all-gather.2
where the time goes:
time: 159 us; the launch traced here: 158 us
  starting transfers between devices  63.4 us (40%)
  waiting for transfers between devices  41.4 us (26%)
  between operations  18.3 us (12%)
  blocking collectives  15.3 us (10%)
  Pallas kernels  12.2 us (8%)
  local copies, waits for them, and re-layouts  5.97 us (4%)
    all_to_all x1, starting transfers between devices, local(): arrived = lax.all_to_all(outgoing, ('core', 'x', 'y'), 0, 0, tiled=True)  18.4 us
    all_to_all x1, blocking collectives, spread(): lax.all_to_all(jnp.broadcast_to(x[None], (count,) + x.shape), axis, 0, 0,...  15.3 us
    all_to_all x1, waiting for transfers between devices, spread(): lax.all_to_all(jnp.broadcast_to(x[None], (count,) + x.shape), axis, 0, 0,...  14.4 us
    all_to_all x1, starting transfers between devices, local(): previous = lax.all_to_all(held, Z, 0, 0, tiled=True)  11.9 us
    all_to_all x1, waiting for transfers between devices, local(): arrived = lax.all_to_all(outgoing, ('core', 'x', 'y'), 0, 0, tiled=True)  8.3 us
    all_to_all x1, waiting for transfers between devices, local(): previous = lax.all_to_all(held, Z, 0, 0, tiled=True)  8.27 us
    ppermute x1, starting transfers between devices, local(): far = lax.ppermute(near, 'core', [(0, 1), (1, 0)])  6.86 us
    pallas_call x1, Pallas kernels, polynomials(): pl.pallas_call(poly_kernel, out_shape=(poly, poly), in_specs=[vmem], out_...  5.55 us
  transfers between devices with their start and end apart: 12, of which 7 were waited for; matrix products, arithmetic and copies ran while one was open for 4% of the time, Pallas kernels for 5%

commit v1 on v0

--- a/solution.py
+++ b/solution.py
@@ -285,12 +285,10 @@
     back = [(k, (k - 1) % NX) for k in range(NX)]
     left0 = lax.ppermute(block[:RG], "x", ahead)
     right1 = lax.ppermute(block[RG:], "x", back)
-    left0, second_half = lax.optimization_barrier((left0, block[RG:]))
+    left1 = lax.ppermute(block[RG:], "x", ahead)
+    right0 = lax.ppermute(block[:RG], "x", back)
     far0 = lax.ppermute(left0, "x", ahead)
-    left1 = lax.ppermute(second_half, "x", ahead)
-    right1, first_half = lax.optimization_barrier((right1, block[:RG]))
     far1 = lax.ppermute(right1, "x", back)
-    right0 = lax.ppermute(first_half, "x", back)
 
     hits = (owners[None, :] == own_index) & (
         slots[None, :] == jnp.arange(DEPTH, dtype=jnp.int32)[:, None]

time: 159 us -> 154 us (0.969)
  waiting for transfers between devices: 41.4 us -> 36.9 us
    ppermute x2, waiting for transfers between devices: 7.74 us -> 0.01 us  [the longest x1 0.01 us: local(): left1 = lax.ppermute(block[RG:], 'x', ahead)]
    ppermute x1, waiting for transfers between devices: 0.01 us -> 2.69 us  [local(): far0 = lax.ppermute(left0, 'x', ahead)]
    ppermute x1, waiting for transfers between devices: 0.01 us -> 1.76 us  [local(): far1 = lax.ppermute(right1, 'x', back)]
  transfers between devices with their start and end apart: 12 -> 12, of which waited for: 7 -> 6; matrix products, arithmetic and copies ran while one was open for 4% -> 4% of each run, Pallas kernels for 5% -> 5%
where the time goes in v1:
time: 154 us; the launch traced here: 153 us
  starting transfers between devices  62.7 us (41%)
  waiting for transfers between devices  36.9 us (24%)
  between operations  18.4 us (12%)
  blocking collectives  15.3 us (10%)
  Pallas kernels  12.2 us (8%)
  local copies, waits for them, and re-layouts  5.97 us (4%)
    all_to_all x1, starting transfers between devices, local(): arrived = lax.all_to_all(outgoing, ('core', 'x', 'y'), 0, 0, tiled=True)  18.4 us
    all_to_all x1, blocking collectives, spread(): lax.all_to_all(jnp.broadcast_to(x[None], (count,) + x.shape), axis, 0, 0,...  15.3 us
    all_to_all x1, waiting for transfers between devices, spread(): lax.all_to_all(jnp.broadcast_to(x[None], (count,) + x.shape), axis, 0, 0,...  14.4 us
    all_to_all x1, starting transfers between devices, local(): previous = lax.all_to_all(held, Z, 0, 0, tiled=True)  11.9 us
    all_to_all x1, waiting for transfers between devices, local(): arrived = lax.all_to_all(outgoing, ('core', 'x', 'y'), 0, 0, tiled=True)  8.3 us
    all_to_all x1, waiting for transfers between devices, local(): previous = lax.all_to_all(held, Z, 0, 0, tiled=True)  8.27 us
    ppermute x1, starting transfers between devices, local(): far = lax.ppermute(near, 'core', [(0, 1), (1, 0)])  6.58 us
    pallas_call x1, Pallas kernels, polynomials(): pl.pallas_call(poly_kernel, out_shape=(poly, poly), in_specs=[vmem], out_...  5.56 us
  transfers between devices with their start and end apart: 12, of which 6 were waited for; matrix products, arithmetic and copies ran while one was open for 4% of the time, Pallas kernels for 5%

profile of v1, /device:TPU:1, one launch (start us, length us, event | category | flops | bytes accessed | tf_op | source)
XLA Modules:
  0.0 152.7 jit_solution(5395194236896010390)
XLA Ops:
  7.2 0.0 copy-start
  7.2 0.0 copy-start.3
  7.2 0.0 all-gather.3.cloned.1.call-start
  7.2 0.9 copy-done
  8.1 0.7 constant_dynamic-slice_fusion
  8.8 0.0 all-gather.3.cloned.1.call-update
  8.8 0.0 copy-start.4
  8.8 18.4 %all-to-all-start = ((bf16[64,16,128]{2,1,0:T(8,128)(2,1)}), bf16[64,16,128]{2,1,0:T(8,128)(2,1)S(1)}, u32[]{:S(2)}, u32[]{:S(2)}) async-start(bf16[64,16,128]{2,1,0:T(8,128)(2,1)} %bitcast.27), calls=%async_computation | async-start | bytes 524288 | tf_op jit(solution)/shard_map/all_to_all | solution.py:278
  27.3 0.9 convert_reduce_fusion.1
  28.2 0.6 dynamic_slice.17
  30.8 0.9 fusion
  31.7 0.6 copy.9
  32.3 8.3 %all-to-all-done = bf16[64,16,128]{2,1,0:T(8,128)(2,1)S(1)} async-done(((bf16[64,16,128]{2,1,0:T(8,128)(2,1)}), bf16[64,16,128]{2,1,0:T(8,128)(2,1)S(1)}, u32[]{:S(2)}, u32[]{:S(2)}) %all-to-all-start) | async-done | bytes 262176 | tf_op jit(solution)/shard_map/all_to_all | solution.py:278
  40.6 11.9 %all-to-all-start.1 = ((bf16[16,16,128]{2,1,0:T(8,128)(2,1)}), bf16[16,16,128]{2,1,0:T(8,128)(2,1)S(1)}, u32[]{:S(2)}, u32[]{:S(2)}) async-start(bf16[16,16,128]{2,1,0:T(8,128)(2,1)} %copy.9), calls=%async_computation.1 | async-start | bytes 131072 | tf_op jit(solution)/shard_map/all_to_all | solution.py:274
  52.5 1.3 dynamic_slice.19
  55.9 0.1 convert_reduce_fusion
  56.0 8.3 %all-to-all-done.1 = bf16[16,16,128]{2,1,0:T(8,128)(2,1)S(1)} async-done(((bf16[16,16,128]{2,1,0:T(8,128)(2,1)}), bf16[16,16,128]{2,1,0:T(8,128)(2,1)S(1)}, u32[]{:S(2)}, u32[]{:S(2)}) %all-to-all-start.1) | async-done | bytes 65568 | tf_op jit(solution)/shard_map/all_to_all | solution.py:274
  64.3 15.3 %all_to_all.20 = bf16[16,16,128]{2,1,0:T(8,128)(2,1)S(1)} all-to-all(bf16[16,16,128]{2,1,0:T(8,128)(2,1)S(1)} %broadcast_in_dim.22), channel_id=1, replica_groups=mesh['y'=8,'x'=4,'core'=2,'fsdp'=16] {'fsdp'}, dimensions={0} | all-to-all | bytes 131072 | tf_op jit(solution)/shard_map/all_to_all | solution.py:249
  79.6 0.9 broadcast_in_dim.23
  80.5 4.0 %all-to-all-start.3 = ((bf16[8,16,16,128]{3,2,1,0:T(8,128)(2,1)}), bf16[8,16,16,128]{3,2,1,0:T(8,128)(2,1)S(1)}, u32[]{:S(2)}, u32[]{:S(2)}) async-start(bf16[8,16,16,128]{3,2,1,0:T(8,128)(2,1)} %broadcast_in_dim.23), calls=%async_computation.3 | async-start | bytes 1048576 | tf_op jit(solution)/shard_map/all_to_all | solution.py:249
  84.5 0.0 copy-done.3
  84.5 14.4 %all-to-all-done.3.own_ref = bf16[8,16,16,128]{3,2,1,0:T(8,128)(2,1)S(1)} async-done(((bf16[8,16,16,128]{3,2,1,0:T(8,128)(2,1)}), bf16[8,16,16,128]{3,2,1,0:T(8,128)(2,1)S(1)}, u32[]{:S(2)}, u32[]{:S(2)}) %all-to-all-start.3) | async-done | bytes 524320 | tf_op jit(solution)/shard_map/all_to_all | solution.py:249
  98.9 1.9 %collective-permute-start = (bf16[4,16,16,128]{3,2,1,0:T(8,128)(2,1)S(1)}, bf16[4,16,16,128]{3,2,1,0:T(8,128)(2,1)S(1)}, u32[]{:S(2)}, u32[]{:S(2)}) collective-permute-start(bf16[4,16,16,128]{3,2,1,0:T(8,128)(2,1)S(1)} %get-tuple-element.29), channel_id=1, source_target_pairs={{0,32},{32,64},{64,96},{96,0},{1,33},{33,65},{65,97},{97,1},{2,34}... | collective-permute-start | bytes 786440 | tf_op jit(solution)/shard_map/ppermute | solution.py:286
  100.8 4.9 %collective-permute-start.3 = (bf16[4,16,16,128]{3,2,1,0:T(8,128)(2,1)S(1)}, bf16[4,16,16,128]{3,2,1,0:T(8,128)(2,1)S(1)}, u32[]{:S(2)}, u32[]{:S(2)}) collective-permute-start(bf16[4,16,16,128]{3,2,1,0:T(8,128)(2,1)S(1)} %get-tuple-element.28), channel_id=1, source_target_pairs={{0,96},{32,0},{64,32},{96,64},{1,97},{33,1},{65,33},{97,65},{2,98}... | collective-permute-start | bytes 786440 | tf_op jit(solution)/shard_map/ppermute | solution.py:287
  105.8 0.1 convert_reduce_fusion.2
  105.9 1.9 %collective-permute-start.1 = (bf16[4,16,16,128]{3,2,1,0:T(8,128)(2,1)S(1)}, bf16[4,16,16,128]{3,2,1,0:T(8,128)(2,1)S(1)}, u32[]{:S(2)}, u32[]{:S(2)}) collective-permute-start(bf16[4,16,16,128]{3,2,1,0:T(8,128)(2,1)S(1)} %get-tuple-element.28), channel_id=1, source_target_pairs={{0,32},{32,64},{64,96},{96,0},{1,33},{33,65},{65,97},{97,1},{2,34}... | collective-permute-start | bytes 786440 | tf_op jit(solution)/shard_map/ppermute | solution.py:288
  107.9 4.6 %collective-permute-start.5 = (bf16[4,16,16,128]{3,2,1,0:T(8,128)(2,1)S(1)}, bf16[4,16,16,128]{3,2,1,0:T(8,128)(2,1)S(1)}, u32[]{:S(2)}, u32[]{:S(2)}) collective-permute-start(bf16[4,16,16,128]{3,2,1,0:T(8,128)(2,1)S(1)} %get-tuple-element.29), channel_id=1, source_target_pairs={{0,96},{32,0},{64,32},{96,64},{1,97},{33,1},{65,33},{97,65},{2,98}... | collective-permute-start | bytes 786440 | tf_op jit(solution)/shard_map/ppermute | solution.py:289
  112.5 0.0 collective-permute-done.refs_0_
  112.5 1.9 %collective-permute-start.2 = (bf16[4,16,16,128]{3,2,1,0:T(8,128)(2,1)S(1)}, bf16[4,16,16,128]{3,2,1,0:T(8,128)(2,1)S(1)}, u32[]{:S(2)}, u32[]{:S(2)}) collective-permute-start(bf16[4,16,16,128]{3,2,1,0:T(8,128)(2,1)S(1)} %collective-permute-done.refs_0_), channel_id=1, source_target_pairs={{0,32},{32,64},{64,96},{96,0},{1,33},{33,65},{65,97},{97,1},{2,34}... | collective-permute-start | bytes 786440 | tf_op jit(solution)/shard_map/ppermute | solution.py:290
  114.4 0.0 collective-permute-done.3.refs_5_
  114.4 4.6 %collective-permute-start.4 = (bf16[4,16,16,128]{3,2,1,0:T(8,128)(2,1)S(1)}, bf16[4,16,16,128]{3,2,1,0:T(8,128)(2,1)S(1)}, u32[]{:S(2)}, u32[]{:S(2)}) collective-permute-start(bf16[4,16,16,128]{3,2,1,0:T(8,128)(2,1)S(1)} %collective-permute-done.3.refs_5_), channel_id=1, source_target_pairs={{0,96},{32,0},{64,32},{96,64},{1,97},{33,1},{65,33},{97,65},{2,98}... | collective-permute-start | bytes 786440 | tf_op jit(solution)/shard_map/ppermute | solution.py:291
  119.0 0.0 copy-done.4
  119.0 0.1 pad_add_fusion.index_ref
  119.1 2.7 %collective-permute-done.2.refs_2_ = bf16[4,16,16,128]{3,2,1,0:T(8,128)(2,1)S(1)} collective-permute-done((bf16[4,16,16,128]{3,2,1,0:T(8,128)(2,1)S(1)}, bf16[4,16,16,128]{3,2,1,0:T(8,128)(2,1)S(1)}, u32[]{:S(2)}, u32[]{:S(2)}) %collective-permute-start.2) | collective-permute-done | bytes 262176 | tf_op jit(solution)/shard_map/ppermute | solution.py:290
  121.8 1.8 %collective-permute-done.4.refs_3_ = bf16[4,16,16,128]{3,2,1,0:T(8,128)(2,1)S(1)} collective-permute-done((bf16[4,16,16,128]{3,2,1,0:T(8,128)(2,1)S(1)}, bf16[4,16,16,128]{3,2,1,0:T(8,128)(2,1)S(1)}, u32[]{:S(2)}, u32[]{:S(2)}) %collective-permute-start.4) | collective-permute-done | bytes 262176 | tf_op jit(solution)/shard_map/ppermute | solution.py:291
  123.5 0.0 collective-permute-done.1.refs_1_
  123.5 0.0 collective-permute-done.5.refs_4_
  123.5 1.0 assemble.1
  124.5 6.6 %collective-permute-start.6 = (bf16[4,64,2048]{2,1,0:T(8,128)(2,1)S(1)}, bf16[4,64,2048]{2,1,0:T(8,128)(2,1)S(1)}, u32[]{:S(2)}, u32[]{:S(2)}) collective-permute-start(bf16[4,64,2048]{2,1,0:T(8,128)(2,1)S(1)} %get-tuple-element.19.near_ref), channel_id=1, source_target_pairs={{0,16},{16,0},{1,17},{17,1},{2,18},{18,2},{3,19},{19,3},{4,20},{20... | collective-permute-start | bytes 3145736 | tf_op jit(solution)/shard_map/ppermute | solution.py:308
  131.1 0.0 copy-start.2
  131.1 5.6 %polynomials.1 = (bf16[2,256,256]{2,1,0:T(8,128)(2,1)S(1)}, bf16[2,256,256]{2,1,0:T(8,128)(2,1)S(1)}) custom-call(bf16[512,2048]{1,0:T(8,128)(2,1)S(1)} %bitcast.25), custom_call_target="tpu_custom_call" | custom-call | flops 8000000000 | bytes 4194304 | tf_op jit(solution)/shard_map/polynomials/pallas_call | solution.py:118
  136.7 0.0 collective-permute-done.6.far_ref
  136.7 0.0 copy-start.1
  136.7 1.7 %update_weights.1.half_ref = bf16[8,64,2048]{2,1,0:T(8,128)(2,1)S(1)} custom-call(bf16[512,2048]{1,0:T(8,128)(2,1)S(1)} %bitcast.26, bf16[2,256,256]{2,1,0:T(8,128)(2,1)S(1)} %get-tuple-element.20.high_ref, bf16[2,256,256]{2,1,0:T(8,128)(2,1)S(1)} %get-tuple-element.21.low_ref, bf16[16,8,64,128]{3,2,1,0:T(8,128)(2,1)S(1)} %bitcast.24), custom_call_target="tpu_custom_call" | custom-call | flops 2000000000 | bytes 6291456 | tf_op jit(solution)/shard_map/update_weights/pallas_call | solution.py:149
  138.5 1.9 %collective-permute-start.7 = (bf16[8,64,2048]{2,1,0:T(8,128)(2,1)S(1)}, bf16[8,64,2048]{2,1,0:T(8,128)(2,1)S(1)}, u32[]{:S(2)}, u32[]{:S(2)}) collective-permute-start(bf16[8,64,2048]{2,1,0:T(8,128)(2,1)S(1)} %update_weights.1.half_ref), channel_id=1, source_target_pairs={{0,16},{16,0},{1,17},{17,1},{2,18},{18,2},{3,19},{19,3},{4,20},{20... | collective-permute-start | bytes 6291464 | tf_op jit(solution)/shard_map/ppermute | solution.py:312
  140.4 2.6 %update_momentum.1 = (f32[4,64,2048]{2,1,0:T(8,128)}, bf16[16,64,2048]{2,1,0:T(8,128)(2,1)}) custom-call(s32[1]{0:T(128)} %bitcast.core_ref, s32[4]{0:T(128)S(1)} %get-tuple-element.30.source_ref, bf16[8,64,2048]{2,1,0:T(8,128)(2,1)S(1)} %update_weights.1.half_ref, bf16[4,64,2048]{2,1,0:T(8,128)(2,1)S(1)} %get-tuple-element.19.near_ref, ...), custom_call_target="tpu_custom_call" | custom-call | flops 4000000 | bytes 10485760 | tf_op jit(solution)/shard_map/update_momentum/pallas_call | solution.py:227
  143.0 1.5 collective-permute-done.7.other_ref
  144.5 1.3 join_halves.1
  (10 shorter events, 0.1 us)
Async XLA Ops:
  7.2 1.0 copy-start
  7.2 77.3 %copy-start.3 = (s32[16]{0:T(128)S(1)}, s32[16]{0:T(128)}, u32[]{:S(2)}) copy-start(s32[16]{0:T(128)} %param.8) | copy-start | bytes 196
  7.2 116.3 %all-gather.3.cloned.1.call-start = ((), (), s32[]{:S(2)}) async-start(), calls=%async_computation.4 | async-start | bytes 2228224 | tf_op jit(solution)/shard_map/all_gather | solution.py:265
  8.8 110.2 %copy-start.4 = (s32[4]{0:T(128)S(1)}, s32[4]{0:T(128)}, u32[]{:S(2)}) copy-start(s32[4]{0:T(128)} %constant.93.clone) | copy-start | bytes 52
  8.8 31.8 %all-to-all-start = ((bf16[64,16,128]{2,1,0:T(8,128)(2,1)}), bf16[64,16,128]{2,1,0:T(8,128)(2,1)S(1)}, u32[]{:S(2)}, u32[]{:S(2)}) async-start(bf16[64,16,128]{2,1,0:T(8,128)(2,1)} %bitcast.27), calls=%async_computation | async-start | bytes 524288 | tf_op jit(solution)/shard_map/all_to_all | solution.py:278
  40.6 23.6 %all-to-all-start.1 = ((bf16[16,16,128]{2,1,0:T(8,128)(2,1)}), bf16[16,16,128]{2,1,0:T(8,128)(2,1)S(1)}, u32[]{:S(2)}, u32[]{:S(2)}) async-start(bf16[16,16,128]{2,1,0:T(8,128)(2,1)} %copy.9), calls=%async_computation.1 | async-start | bytes 131072 | tf_op jit(solution)/shard_map/all_to_all | solution.py:274
  80.5 18.4 %all-to-all-start.3 = ((bf16[8,16,16,128]{3,2,1,0:T(8,128)(2,1)}), bf16[8,16,16,128]{3,2,1,0:T(8,128)(2,1)S(1)}, u32[]{:S(2)}, u32[]{:S(2)}) async-start(bf16[8,16,16,128]{3,2,1,0:T(8,128)(2,1)} %broadcast_in_dim.23), calls=%async_computation.3 | async-start | bytes 1048576 | tf_op jit(solution)/shard_map/all_to_all | solution.py:249
  98.9 13.5 %collective-permute-start = (bf16[4,16,16,128]{3,2,1,0:T(8,128)(2,1)S(1)}, bf16[4,16,16,128]{3,2,1,0:T(8,128)(2,1)S(1)}, u32[]{:S(2)}, u32[]{:S(2)}) collective-permute-start(bf16[4,16,16,128]{3,2,1,0:T(8,128)(2,1)S(1)} %get-tuple-element.29), channel_id=1, source_target_pairs={{0,32},{32,64},{64,96},{96,0},{1,33},{33,65},{65,97},{97,1},{2,34}... | collective-permute-start | bytes 786440 | tf_op jit(solution)/shard_map/ppermute | solution.py:286
  100.8 13.6 %collective-permute-start.3 = (bf16[4,16,16,128]{3,2,1,0:T(8,128)(2,1)S(1)}, bf16[4,16,16,128]{3,2,1,0:T(8,128)(2,1)S(1)}, u32[]{:S(2)}, u32[]{:S(2)}) collective-permute-start(bf16[4,16,16,128]{3,2,1,0:T(8,128)(2,1)S(1)} %get-tuple-element.28), channel_id=1, source_target_pairs={{0,96},{32,0},{64,32},{96,64},{1,97},{33,1},{65,33},{97,65},{2,98}... | collective-permute-start | bytes 786440 | tf_op jit(solution)/shard_map/ppermute | solution.py:287
  105.9 17.6 %collective-permute-start.1 = (bf16[4,16,16,128]{3,2,1,0:T(8,128)(2,1)S(1)}, bf16[4,16,16,128]{3,2,1,0:T(8,128)(2,1)S(1)}, u32[]{:S(2)}, u32[]{:S(2)}) collective-permute-start(bf16[4,16,16,128]{3,2,1,0:T(8,128)(2,1)S(1)} %get-tuple-element.28), channel_id=1, source_target_pairs={{0,32},{32,64},{64,96},{96,0},{1,33},{33,65},{65,97},{97,1},{2,34}... | collective-permute-start | bytes 786440 | tf_op jit(solution)/shard_map/ppermute | solution.py:288
  107.9 15.7 %collective-permute-start.5 = (bf16[4,16,16,128]{3,2,1,0:T(8,128)(2,1)S(1)}, bf16[4,16,16,128]{3,2,1,0:T(8,128)(2,1)S(1)}, u32[]{:S(2)}, u32[]{:S(2)}) collective-permute-start(bf16[4,16,16,128]{3,2,1,0:T(8,128)(2,1)S(1)} %get-tuple-element.29), channel_id=1, source_target_pairs={{0,96},{32,0},{64,32},{96,64},{1,97},{33,1},{65,33},{97,65},{2,98}... | collective-permute-start | bytes 786440 | tf_op jit(solution)/shard_map/ppermute | solution.py:289
  112.5 9.3 %collective-permute-start.2 = (bf16[4,16,16,128]{3,2,1,0:T(8,128)(2,1)S(1)}, bf16[4,16,16,128]{3,2,1,0:T(8,128)(2,1)S(1)}, u32[]{:S(2)}, u32[]{:S(2)}) collective-permute-start(bf16[4,16,16,128]{3,2,1,0:T(8,128)(2,1)S(1)} %collective-permute-done.refs_0_), channel_id=1, source_target_pairs={{0,32},{32,64},{64,96},{96,0},{1,33},{33,65},{65,97},{97,1},{2,34}... | collective-permute-start | bytes 786440 | tf_op jit(solution)/shard_map/ppermute | solution.py:290
  114.4 9.1 %collective-permute-start.4 = (bf16[4,16,16,128]{3,2,1,0:T(8,128)(2,1)S(1)}, bf16[4,16,16,128]{3,2,1,0:T(8,128)(2,1)S(1)}, u32[]{:S(2)}, u32[]{:S(2)}) collective-permute-start(bf16[4,16,16,128]{3,2,1,0:T(8,128)(2,1)S(1)} %collective-permute-done.3.refs_5_), channel_id=1, source_target_pairs={{0,96},{32,0},{64,32},{96,64},{1,97},{33,1},{65,33},{97,65},{2,98}... | collective-permute-start | bytes 786440 | tf_op jit(solution)/shard_map/ppermute | solution.py:291
  124.5 12.2 %collective-permute-start.6 = (bf16[4,64,2048]{2,1,0:T(8,128)(2,1)S(1)}, bf16[4,64,2048]{2,1,0:T(8,128)(2,1)S(1)}, u32[]{:S(2)}, u32[]{:S(2)}) collective-permute-start(bf16[4,64,2048]{2,1,0:T(8,128)(2,1)S(1)} %get-tuple-element.19.near_ref), channel_id=1, source_target_pairs={{0,16},{16,0},{1,17},{17,1},{2,18},{18,2},{3,19},{19,3},{4,20},{20... | collective-permute-start | bytes 3145736 | tf_op jit(solution)/shard_map/ppermute | solution.py:308
  131.1 5.6 %copy-start.2 = (bf16[128,64,128]{2,1,0:T(8,128)(2,1)S(1)}, bf16[128,64,128]{2,1,0:T(8,128)(2,1)}, u32[]{:S(2)}) copy-start(bf16[128,64,128]{2,1,0:T(8,128)(2,1)} %all-gather.3.cloned.1.call-done) | copy-start | bytes 6291460
  136.7 3.6 %copy-start.1 = (f32[1,4,64,2048]{3,2,1,0:T(8,128)S(1)}, f32[1,4,64,2048]{3,2,1,0:T(8,128)}, u32[]{:S(2)}) copy-start(f32[1,4,64,2048]{3,2,1,0:T(8,128)} %param.7) | copy-start | bytes 6291460
  138.5 6.1 %collective-permute-start.7 = (bf16[8,64,2048]{2,1,0:T(8,128)(2,1)S(1)}, bf16[8,64,2048]{2,1,0:T(8,128)(2,1)S(1)}, u32[]{:S(2)}, u32[]{:S(2)}) collective-permute-start(bf16[8,64,2048]{2,1,0:T(8,128)(2,1)S(1)} %update_weights.1.half_ref), channel_id=1, source_target_pairs={{0,16},{16,0},{1,17},{17,1},{2,18},{18,2},{3,19},{19,3},{4,20},{20... | collective-permute-start | bytes 6291464 | tf_op jit(solution)/shard_map/ppermute | solution.py:312
Sparse Core Ops, SparseCore 0:
  11.3 79.5 all-gather.2

commit v2 on v1

--- a/solution.py
+++ b/solution.py
@@ -281,14 +281,15 @@
 
     block = spread(initial.astype(jnp.bfloat16), Z, NZ)
     block = spread(block, "y", NY)
-    ahead = [(k, (k + 1) % NX) for k in range(NX)]
-    back = [(k, (k - 1) % NX) for k in range(NX)]
-    left0 = lax.ppermute(block[:RG], "x", ahead)
-    right1 = lax.ppermute(block[RG:], "x", back)
-    left1 = lax.ppermute(block[RG:], "x", ahead)
-    right0 = lax.ppermute(block[:RG], "x", back)
-    far0 = lax.ppermute(left0, "x", ahead)
-    far1 = lax.ppermute(right1, "x", back)
+    ring = [(k, c, 1 - 2 * c) for k in range(NX) for c in range(NC)]
+    ahead = [(NC * k + c, NC * ((k + way) % NX) + c) for k, c, way in ring]
+    back = [(NC * k + c, NC * ((k - way) % NX) + c) for k, c, way in ring]
+    left0 = lax.ppermute(block[:RG], ("x", "core"), ahead)
+    right1 = lax.ppermute(block[RG:], ("x", "core"), back)
+    left1 = lax.ppermute(block[RG:], ("x", "core"), ahead)
+    right0 = lax.ppermute(block[:RG], ("x", "core"), back)
+    far0 = lax.ppermute(left0, ("x", "core"), ahead)
+    far1 = lax.ppermute(right1, ("x", "core"), back)
 
     hits = (owners[None, :] == own_index) & (
         slots[None, :] == jnp.arange(DEPTH, dtype=jnp.int32)[:, None]
@@ -298,7 +299,7 @@
     in_half = (which >= first) & (which < first + HALF)
     source = jnp.where(present > 0, jnp.where(in_half, 1, 2), 0).astype(jnp.int32)
     far0, far1, weights_half = lax.optimization_barrier((far0, far1, weights_half))
-    places = (x + jnp.array([0, NX - 1, 2, 1], jnp.int32)) % NX
+    places = (x + (1 - 2 * core) * jnp.array([0, -1, 2, 1], jnp.int32) + NX) % NX
     index = jnp.concatenate([places, which % HALF]).astype(jnp.int32)
     xs, near = assemble(index, block, left0, left1, far0, far1, right0, right1)
 

time: 154 us -> 154 us (level)
  waiting for transfers between devices: 36.9 us -> 41.3 us
  starting transfers between devices: 62.7 us -> 59 us
    ppermute x6, waiting for transfers between devices: 4.46 us -> 8.79 us  [the longest x1 5.02 us: local(): far1 = lax.ppermute(right1, ('x', 'core'), back)]
    ppermute x1, starting transfers between devices: 6.58 us -> 2.93 us  [local(): far = lax.ppermute(near, 'core', [(0, 1), (1, 0)])]
where the time goes in v2:
time: 154 us; the launch traced here: 153 us
  starting transfers between devices  59 us (38%)
  waiting for transfers between devices  41.3 us (27%)
  between operations  18.4 us (12%)
  blocking collectives  15.3 us (10%)
  Pallas kernels  12.2 us (8%)
  local copies, waits for them, and re-layouts  5.97 us (4%)
    all_to_all x1, starting transfers between devices, local(): arrived = lax.all_to_all(outgoing, ('core', 'x', 'y'), 0, 0, tiled=True)  18.4 us
    all_to_all x1, blocking collectives, spread(): lax.all_to_all(jnp.broadcast_to(x[None], (count,) + x.shape), axis, 0, 0,...  15.3 us
    all_to_all x1, waiting for transfers between devices, spread(): lax.all_to_all(jnp.broadcast_to(x[None], (count,) + x.shape), axis, 0, 0,...  14.4 us
    all_to_all x1, starting transfers between devices, local(): previous = lax.all_to_all(held, Z, 0, 0, tiled=True)  11.9 us
    all_to_all x1, waiting for transfers between devices, local(): arrived = lax.all_to_all(outgoing, ('core', 'x', 'y'), 0, 0, tiled=True)  8.3 us
    all_to_all x1, waiting for transfers between devices, local(): previous = lax.all_to_all(held, Z, 0, 0, tiled=True)  8.27 us
    pallas_call x1, Pallas kernels, polynomials(): pl.pallas_call(poly_kernel, out_shape=(poly, poly), in_specs=[vmem], out_...  5.53 us
    ppermute x1, waiting for transfers between devices, local(): far1 = lax.ppermute(right1, ('x', 'core'), back)  5.02 us
  transfers between devices with their start and end apart: 12, of which 6 were waited for; matrix products, arithmetic and copies ran while one was open for 4% of the time, Pallas kernels for 5%

profile of v2, /device:TPU:1, one launch (start us, length us, event | category | flops | bytes accessed | tf_op | source)
XLA Modules:
  0.0 153.4 jit_solution(13026426551801419323)
XLA Ops:
  7.2 0.0 copy-start
  7.2 0.0 copy-start.4
  7.2 0.0 all-gather.3.cloned.1.call-start
  7.2 0.9 copy-done
  8.1 0.7 constant_dynamic-slice_fusion
  8.8 0.0 all-gather.3.cloned.1.call-update
  8.8 0.0 copy-start.3
  8.8 18.4 %all-to-all-start = ((bf16[64,16,128]{2,1,0:T(8,128)(2,1)}), bf16[64,16,128]{2,1,0:T(8,128)(2,1)S(1)}, u32[]{:S(2)}, u32[]{:S(2)}) async-start(bf16[64,16,128]{2,1,0:T(8,128)(2,1)} %bitcast.27), calls=%async_computation | async-start | bytes 524288 | tf_op jit(solution)/shard_map/all_to_all | solution.py:278
  27.3 0.9 convert_reduce_fusion.1
  28.2 0.6 dynamic_slice.17
  30.8 0.9 fusion
  31.7 0.6 copy.9
  32.3 8.3 %all-to-all-done = bf16[64,16,128]{2,1,0:T(8,128)(2,1)S(1)} async-done(((bf16[64,16,128]{2,1,0:T(8,128)(2,1)}), bf16[64,16,128]{2,1,0:T(8,128)(2,1)S(1)}, u32[]{:S(2)}, u32[]{:S(2)}) %all-to-all-start) | async-done | bytes 262176 | tf_op jit(solution)/shard_map/all_to_all | solution.py:278
  40.6 11.9 %all-to-all-start.1 = ((bf16[16,16,128]{2,1,0:T(8,128)(2,1)}), bf16[16,16,128]{2,1,0:T(8,128)(2,1)S(1)}, u32[]{:S(2)}, u32[]{:S(2)}) async-start(bf16[16,16,128]{2,1,0:T(8,128)(2,1)} %copy.9), calls=%async_computation.1 | async-start | bytes 131072 | tf_op jit(solution)/shard_map/all_to_all | solution.py:274
  52.5 1.3 dynamic_slice.19
  55.9 0.1 convert_reduce_fusion
  56.0 8.3 %all-to-all-done.1 = bf16[16,16,128]{2,1,0:T(8,128)(2,1)S(1)} async-done(((bf16[16,16,128]{2,1,0:T(8,128)(2,1)}), bf16[16,16,128]{2,1,0:T(8,128)(2,1)S(1)}, u32[]{:S(2)}, u32[]{:S(2)}) %all-to-all-start.1) | async-done | bytes 65568 | tf_op jit(solution)/shard_map/all_to_all | solution.py:274
  64.3 15.3 %all_to_all.20 = bf16[16,16,128]{2,1,0:T(8,128)(2,1)S(1)} all-to-all(bf16[16,16,128]{2,1,0:T(8,128)(2,1)S(1)} %broadcast_in_dim.22), channel_id=1, replica_groups=mesh['y'=8,'x'=4,'core'=2,'fsdp'=16] {'fsdp'}, dimensions={0} | all-to-all | bytes 131072 | tf_op jit(solution)/shard_map/all_to_all | solution.py:249
  79.6 0.9 broadcast_in_dim.23
  80.5 4.0 %all-to-all-start.3 = ((bf16[8,16,16,128]{3,2,1,0:T(8,128)(2,1)}), bf16[8,16,16,128]{3,2,1,0:T(8,128)(2,1)S(1)}, u32[]{:S(2)}, u32[]{:S(2)}) async-start(bf16[8,16,16,128]{3,2,1,0:T(8,128)(2,1)} %broadcast_in_dim.23), calls=%async_computation.3 | async-start | bytes 1048576 | tf_op jit(solution)/shard_map/all_to_all | solution.py:249
  84.5 0.0 copy-done.4
  84.5 14.4 %all-to-all-done.3.own_ref = bf16[8,16,16,128]{3,2,1,0:T(8,128)(2,1)S(1)} async-done(((bf16[8,16,16,128]{3,2,1,0:T(8,128)(2,1)}), bf16[8,16,16,128]{3,2,1,0:T(8,128)(2,1)S(1)}, u32[]{:S(2)}, u32[]{:S(2)}) %all-to-all-start.3) | async-done | bytes 524320 | tf_op jit(solution)/shard_map/all_to_all | solution.py:249
  98.9 4.9 %collective-permute-start = (bf16[4,16,16,128]{3,2,1,0:T(8,128)(2,1)S(1)}, bf16[4,16,16,128]{3,2,1,0:T(8,128)(2,1)S(1)}, u32[]{:S(2)}, u32[]{:S(2)}) collective-permute-start(bf16[4,16,16,128]{3,2,1,0:T(8,128)(2,1)S(1)} %get-tuple-element.29), channel_id=1, source_target_pairs={{0,32},{16,112},{32,64},{48,16},{64,96},{80,48},{96,0},{112,80},{1... | collective-permute-start | bytes 786440 | tf_op jit(solution)/shard_map/ppermute | solution.py:287
  103.8 1.9 %collective-permute-start.3 = (bf16[4,16,16,128]{3,2,1,0:T(8,128)(2,1)S(1)}, bf16[4,16,16,128]{3,2,1,0:T(8,128)(2,1)S(1)}, u32[]{:S(2)}, u32[]{:S(2)}) collective-permute-start(bf16[4,16,16,128]{3,2,1,0:T(8,128)(2,1)S(1)} %get-tuple-element.28), channel_id=1, source_target_pairs={{0,96},{16,48},{32,0},{48,80},{64,32},{80,112},{96,64},{112,16},{1... | collective-permute-start | bytes 786440 | tf_op jit(solution)/shard_map/ppermute | solution.py:288
  105.8 0.1 convert_reduce_fusion.2
  105.9 4.6 %collective-permute-start.1 = (bf16[4,16,16,128]{3,2,1,0:T(8,128)(2,1)S(1)}, bf16[4,16,16,128]{3,2,1,0:T(8,128)(2,1)S(1)}, u32[]{:S(2)}, u32[]{:S(2)}) collective-permute-start(bf16[4,16,16,128]{3,2,1,0:T(8,128)(2,1)S(1)} %get-tuple-element.28), channel_id=1, source_target_pairs={{0,32},{16,112},{32,64},{48,16},{64,96},{80,48},{96,0},{112,80},{1... | collective-permute-start | bytes 786440 | tf_op jit(solution)/shard_map/ppermute | solution.py:289
  110.5 1.9 %collective-permute-start.5 = (bf16[4,16,16,128]{3,2,1,0:T(8,128)(2,1)S(1)}, bf16[4,16,16,128]{3,2,1,0:T(8,128)(2,1)S(1)}, u32[]{:S(2)}, u32[]{:S(2)}) collective-permute-start(bf16[4,16,16,128]{3,2,1,0:T(8,128)(2,1)S(1)} %get-tuple-element.29), channel_id=1, source_target_pairs={{0,96},{16,48},{32,0},{48,80},{64,32},{80,112},{96,64},{112,16},{1... | collective-permute-start | bytes 786440 | tf_op jit(solution)/shard_map/ppermute | solution.py:290
  112.5 0.0 collective-permute-done.refs_0_
  112.5 4.6 %collective-permute-start.2 = (bf16[4,16,16,128]{3,2,1,0:T(8,128)(2,1)S(1)}, bf16[4,16,16,128]{3,2,1,0:T(8,128)(2,1)S(1)}, u32[]{:S(2)}, u32[]{:S(2)}) collective-permute-start(bf16[4,16,16,128]{3,2,1,0:T(8,128)(2,1)S(1)} %collective-permute-done.refs_0_), channel_id=1, source_target_pairs={{0,32},{16,112},{32,64},{48,16},{64,96},{80,48},{96,0},{112,80},{1... | collective-permute-start | bytes 786440 | tf_op jit(solution)/shard_map/ppermute | solution.py:291
  117.0 0.0 collective-permute-done.3.refs_5_
  117.1 1.9 %collective-permute-start.4 = (bf16[4,16,16,128]{3,2,1,0:T(8,128)(2,1)S(1)}, bf16[4,16,16,128]{3,2,1,0:T(8,128)(2,1)S(1)}, u32[]{:S(2)}, u32[]{:S(2)}) collective-permute-start(bf16[4,16,16,128]{3,2,1,0:T(8,128)(2,1)S(1)} %collective-permute-done.3.refs_5_), channel_id=1, source_target_pairs={{0,96},{16,48},{32,0},{48,80},{64,32},{80,112},{96,64},{112,16},{1... | collective-permute-start | bytes 786440 | tf_op jit(solution)/shard_map/ppermute | solution.py:292
  119.0 0.0 copy-done.3
  119.0 0.1 pad_add_fusion.index_ref
  119.1 3.8 %collective-permute-done.2.refs_2_ = bf16[4,16,16,128]{3,2,1,0:T(8,128)(2,1)S(1)} collective-permute-done((bf16[4,16,16,128]{3,2,1,0:T(8,128)(2,1)S(1)}, bf16[4,16,16,128]{3,2,1,0:T(8,128)(2,1)S(1)}, u32[]{:S(2)}, u32[]{:S(2)}) %collective-permute-start.2) | collective-permute-done | bytes 262176 | tf_op jit(solution)/shard_map/ppermute | solution.py:291
  122.9 5.0 %collective-permute-done.4.refs_3_ = bf16[4,16,16,128]{3,2,1,0:T(8,128)(2,1)S(1)} collective-permute-done((bf16[4,16,16,128]{3,2,1,0:T(8,128)(2,1)S(1)}, bf16[4,16,16,128]{3,2,1,0:T(8,128)(2,1)S(1)}, u32[]{:S(2)}, u32[]{:S(2)}) %collective-permute-start.4) | collective-permute-done | bytes 262176 | tf_op jit(solution)/shard_map/ppermute | solution.py:292
  127.9 0.0 collective-permute-done.1.refs_1_
  127.9 0.0 collective-permute-done.5.refs_4_
  127.9 1.0 assemble.1
  128.9 2.9 %collective-permute-start.6 = (bf16[4,64,2048]{2,1,0:T(8,128)(2,1)S(1)}, bf16[4,64,2048]{2,1,0:T(8,128)(2,1)S(1)}, u32[]{:S(2)}, u32[]{:S(2)}) collective-permute-start(bf16[4,64,2048]{2,1,0:T(8,128)(2,1)S(1)} %get-tuple-element.19.near_ref), channel_id=1, source_target_pairs={{0,16},{16,0},{1,17},{17,1},{2,18},{18,2},{3,19},{19,3},{4,20},{20... | collective-permute-start | bytes 3145736 | tf_op jit(solution)/shard_map/ppermute | solution.py:309
  131.8 0.0 copy-start.2
  131.8 5.5 %polynomials.1 = (bf16[2,256,256]{2,1,0:T(8,128)(2,1)S(1)}, bf16[2,256,256]{2,1,0:T(8,128)(2,1)S(1)}) custom-call(bf16[512,2048]{1,0:T(8,128)(2,1)S(1)} %bitcast.25), custom_call_target="tpu_custom_call" | custom-call | flops 8000000000 | bytes 4194304 | tf_op jit(solution)/shard_map/polynomials/pallas_call | solution.py:118
  137.4 0.0 collective-permute-done.6.far_ref
  137.4 0.0 copy-start.1
  137.4 1.7 %update_weights.1.half_ref = bf16[8,64,2048]{2,1,0:T(8,128)(2,1)S(1)} custom-call(bf16[512,2048]{1,0:T(8,128)(2,1)S(1)} %bitcast.26, bf16[2,256,256]{2,1,0:T(8,128)(2,1)S(1)} %get-tuple-element.20.high_ref, bf16[2,256,256]{2,1,0:T(8,128)(2,1)S(1)} %get-tuple-element.21.low_ref, bf16[16,8,64,128]{3,2,1,0:T(8,128)(2,1)S(1)} %bitcast.24), custom_call_target="tpu_custom_call" | custom-call | flops 2000000000 | bytes 6291456 | tf_op jit(solution)/shard_map/update_weights/pallas_call | solution.py:149
  139.1 1.9 %collective-permute-start.7 = (bf16[8,64,2048]{2,1,0:T(8,128)(2,1)S(1)}, bf16[8,64,2048]{2,1,0:T(8,128)(2,1)S(1)}, u32[]{:S(2)}, u32[]{:S(2)}) collective-permute-start(bf16[8,64,2048]{2,1,0:T(8,128)(2,1)S(1)} %update_weights.1.half_ref), channel_id=1, source_target_pairs={{0,16},{16,0},{1,17},{17,1},{2,18},{18,2},{3,19},{19,3},{4,20},{20... | collective-permute-start | bytes 6291464 | tf_op jit(solution)/shard_map/ppermute | solution.py:313
  141.1 2.6 %update_momentum.1 = (f32[4,64,2048]{2,1,0:T(8,128)}, bf16[16,64,2048]{2,1,0:T(8,128)(2,1)}) custom-call(s32[1]{0:T(128)} %bitcast.core_ref, s32[4]{0:T(128)S(1)} %get-tuple-element.30.source_ref, bf16[8,64,2048]{2,1,0:T(8,128)(2,1)S(1)} %update_weights.1.half_ref, bf16[4,64,2048]{2,1,0:T(8,128)(2,1)S(1)} %get-tuple-element.19.near_ref, ...), custom_call_target="tpu_custom_call" | custom-call | flops 4000000 | bytes 10485760 | tf_op jit(solution)/shard_map/update_momentum/pallas_call | solution.py:227
  143.7 1.5 collective-permute-done.7.other_ref
  145.2 1.3 join_halves.1
  (10 shorter events, 0.1 us)
Async XLA Ops:
  7.2 1.0 copy-start
  7.2 77.3 %copy-start.4 = (s32[16]{0:T(128)S(1)}, s32[16]{0:T(128)}, u32[]{:S(2)}) copy-start(s32[16]{0:T(128)} %param.8) | copy-start | bytes 196
  7.2 120.7 %all-gather.3.cloned.1.call-start = ((), (), s32[]{:S(2)}) async-start(), calls=%async_computation.4 | async-start | bytes 2228224 | tf_op jit(solution)/shard_map/all_gather | solution.py:265
  8.8 110.2 %copy-start.3 = (s32[4]{0:T(128)S(1)}, s32[4]{0:T(128)}, u32[]{:S(2)}) copy-start(s32[4]{0:T(128)} %constant.94.clone) | copy-start | bytes 52
  8.8 31.8 %all-to-all-start = ((bf16[64,16,128]{2,1,0:T(8,128)(2,1)}), bf16[64,16,128]{2,1,0:T(8,128)(2,1)S(1)}, u32[]{:S(2)}, u32[]{:S(2)}) async-start(bf16[64,16,128]{2,1,0:T(8,128)(2,1)} %bitcast.27), calls=%async_computation | async-start | bytes 524288 | tf_op jit(solution)/shard_map/all_to_all | solution.py:278
  40.6 23.6 %all-to-all-start.1 = ((bf16[16,16,128]{2,1,0:T(8,128)(2,1)}), bf16[16,16,128]{2,1,0:T(8,128)(2,1)S(1)}, u32[]{:S(2)}, u32[]{:S(2)}) async-start(bf16[16,16,128]{2,1,0:T(8,128)(2,1)} %copy.9), calls=%async_computation.1 | async-start | bytes 131072 | tf_op jit(solution)/shard_map/all_to_all | solution.py:274
  80.5 18.4 %all-to-all-start.3 = ((bf16[8,16,16,128]{3,2,1,0:T(8,128)(2,1)}), bf16[8,16,16,128]{3,2,1,0:T(8,128)(2,1)S(1)}, u32[]{:S(2)}, u32[]{:S(2)}) async-start(bf16[8,16,16,128]{3,2,1,0:T(8,128)(2,1)} %broadcast_in_dim.23), calls=%async_computation.3 | async-start | bytes 1048576 | tf_op jit(solution)/shard_map/all_to_all | solution.py:249
  98.9 13.5 %collective-permute-start = (bf16[4,16,16,128]{3,2,1,0:T(8,128)(2,1)S(1)}, bf16[4,16,16,128]{3,2,1,0:T(8,128)(2,1)S(1)}, u32[]{:S(2)}, u32[]{:S(2)}) collective-permute-start(bf16[4,16,16,128]{3,2,1,0:T(8,128)(2,1)S(1)} %get-tuple-element.29), channel_id=1, source_target_pairs={{0,32},{16,112},{32,64},{48,16},{64,96},{80,48},{96,0},{112,80},{1... | collective-permute-start | bytes 786440 | tf_op jit(solution)/shard_map/ppermute | solution.py:287
  103.8 13.2 %collective-permute-start.3 = (bf16[4,16,16,128]{3,2,1,0:T(8,128)(2,1)S(1)}, bf16[4,16,16,128]{3,2,1,0:T(8,128)(2,1)S(1)}, u32[]{:S(2)}, u32[]{:S(2)}) collective-permute-start(bf16[4,16,16,128]{3,2,1,0:T(8,128)(2,1)S(1)} %get-tuple-element.28), channel_id=1, source_target_pairs={{0,96},{16,48},{32,0},{48,80},{64,32},{80,112},{96,64},{112,16},{1... | collective-permute-start | bytes 786440 | tf_op jit(solution)/shard_map/ppermute | solution.py:288
  105.9 21.9 %collective-permute-start.1 = (bf16[4,16,16,128]{3,2,1,0:T(8,128)(2,1)S(1)}, bf16[4,16,16,128]{3,2,1,0:T(8,128)(2,1)S(1)}, u32[]{:S(2)}, u32[]{:S(2)}) collective-permute-start(bf16[4,16,16,128]{3,2,1,0:T(8,128)(2,1)S(1)} %get-tuple-element.28), channel_id=1, source_target_pairs={{0,32},{16,112},{32,64},{48,16},{64,96},{80,48},{96,0},{112,80},{1... | collective-permute-start | bytes 786440 | tf_op jit(solution)/shard_map/ppermute | solution.py:289
  110.5 17.3 %collective-permute-start.5 = (bf16[4,16,16,128]{3,2,1,0:T(8,128)(2,1)S(1)}, bf16[4,16,16,128]{3,2,1,0:T(8,128)(2,1)S(1)}, u32[]{:S(2)}, u32[]{:S(2)}) collective-permute-start(bf16[4,16,16,128]{3,2,1,0:T(8,128)(2,1)S(1)} %get-tuple-element.29), channel_id=1, source_target_pairs={{0,96},{16,48},{32,0},{48,80},{64,32},{80,112},{96,64},{112,16},{1... | collective-permute-start | bytes 786440 | tf_op jit(solution)/shard_map/ppermute | solution.py:290
  112.5 10.4 %collective-permute-start.2 = (bf16[4,16,16,128]{3,2,1,0:T(8,128)(2,1)S(1)}, bf16[4,16,16,128]{3,2,1,0:T(8,128)(2,1)S(1)}, u32[]{:S(2)}, u32[]{:S(2)}) collective-permute-start(bf16[4,16,16,128]{3,2,1,0:T(8,128)(2,1)S(1)} %collective-permute-done.refs_0_), channel_id=1, source_target_pairs={{0,32},{16,112},{32,64},{48,16},{64,96},{80,48},{96,0},{112,80},{1... | collective-permute-start | bytes 786440 | tf_op jit(solution)/shard_map/ppermute | solution.py:291
  117.1 10.8 %collective-permute-start.4 = (bf16[4,16,16,128]{3,2,1,0:T(8,128)(2,1)S(1)}, bf16[4,16,16,128]{3,2,1,0:T(8,128)(2,1)S(1)}, u32[]{:S(2)}, u32[]{:S(2)}) collective-permute-start(bf16[4,16,16,128]{3,2,1,0:T(8,128)(2,1)S(1)} %collective-permute-done.3.refs_5_), channel_id=1, source_target_pairs={{0,96},{16,48},{32,0},{48,80},{64,32},{80,112},{96,64},{112,16},{1... | collective-permute-start | bytes 786440 | tf_op jit(solution)/shard_map/ppermute | solution.py:292
  128.9 8.5 %collective-permute-start.6 = (bf16[4,64,2048]{2,1,0:T(8,128)(2,1)S(1)}, bf16[4,64,2048]{2,1,0:T(8,128)(2,1)S(1)}, u32[]{:S(2)}, u32[]{:S(2)}) collective-permute-start(bf16[4,64,2048]{2,1,0:T(8,128)(2,1)S(1)} %get-tuple-element.19.near_ref), channel_id=1, source_target_pairs={{0,16},{16,0},{1,17},{17,1},{2,18},{18,2},{3,19},{19,3},{4,20},{20... | collective-permute-start | bytes 3145736 | tf_op jit(solution)/shard_map/ppermute | solution.py:309
  131.8 5.6 %copy-start.2 = (bf16[128,64,128]{2,1,0:T(8,128)(2,1)S(1)}, bf16[128,64,128]{2,1,0:T(8,128)(2,1)}, u32[]{:S(2)}) copy-start(bf16[128,64,128]{2,1,0:T(8,128)(2,1)} %all-gather.3.cloned.1.call-done) | copy-start | bytes 6291460
  137.4 3.7 %copy-start.1 = (f32[1,4,64,2048]{3,2,1,0:T(8,128)S(1)}, f32[1,4,64,2048]{3,2,1,0:T(8,128)}, u32[]{:S(2)}) copy-start(f32[1,4,64,2048]{3,2,1,0:T(8,128)} %param.7) | copy-start | bytes 6291460
  139.1 6.1 %collective-permute-start.7 = (bf16[8,64,2048]{2,1,0:T(8,128)(2,1)S(1)}, bf16[8,64,2048]{2,1,0:T(8,128)(2,1)S(1)}, u32[]{:S(2)}, u32[]{:S(2)}) collective-permute-start(bf16[8,64,2048]{2,1,0:T(8,128)(2,1)S(1)} %update_weights.1.half_ref), channel_id=1, source_target_pairs={{0,16},{16,0},{1,17},{17,1},{2,18},{18,2},{3,19},{19,3},{4,20},{20... | collective-permute-start | bytes 6291464 | tf_op jit(solution)/shard_map/ppermute | solution.py:313
Sparse Core Ops, SparseCore 0:
  11.3 79.5 all-gather.2
